TPU v7x, 512 devices: a whole 4x8x8 slice. The times are simulated.
512 devices in a mesh: dp: 512 (over z, y, x, core).
Axes of the slice: x: 4, y: 8, z: 8, core: 2. Of those that a mesh axis runs over, the one named last changes fastest.
Arguments:
- images: float32 [131072, 1152], P('dp'), may hold values from -0.2 to 0.2
- texts: float32 [131072, 1152], P('dp'), may hold values from -0.2 to 0.2
- log_scale: float32 [1], replicated, may hold values from 2 to 2.8
- bias: float32 [1], replicated, may hold values from -3 to -1
Outputs:
- image_grad: float32 [131072, 1152], P('dp')
- text_grad: float32 [131072, 1152], P('dp')
All inputs are finite; a program needn't handle non-finite values.
Results may differ from a plain program's by a relative error of at most 0.00012.
Values sent between devices are 32-bit elements; how exact they have to be, the bound alone decides.
A program may use at most 64 MiB of HBM per device.

v0:
```python
import jax
import jax.numpy as jnp
from jax import lax
from jax.sharding import PartitionSpec as P

STEPS = 4


def passed_along(shard, axis, by):
    peers = lax.axis_size(axis)
    return lax.ppermute(shard, axis, [(i, (i + by) % peers) for i in range(peers)])


def pair_grads(images, visit, scale, offset, first):
    logits = (
        scale
        * lax.dot_general(images, visit, (((1,), (1,)), ((), ())), precision=lax.Precision.HIGHEST)
        + offset
    )
    count = images.shape[0]
    if first:
        diag = jnp.arange(count)[:, None] == jnp.arange(count)[None, :]
        sign = jnp.where(diag, 1.0, -1.0).astype(jnp.float32)
    else:
        sign = -jnp.ones((count, count), jnp.float32)
    return -sign * jax.nn.sigmoid(-sign * logits) * scale


def per_device(images, texts, log_scale, bias):
    scale = jnp.exp(log_scale[0])
    offset = bias[0]
    image_grad = jnp.zeros_like(images)
    visit = texts
    carried = jnp.zeros_like(texts)
    for step in range(STEPS):
        if step > 0:
            visit = passed_along(visit, "dp", 1)
        grads = pair_grads(images, visit, scale, offset, step == 0)
        image_grad = image_grad + jnp.dot(grads, visit, precision=lax.Precision.HIGHEST)
        contrib = lax.dot_general(
            grads, images, (((0,), (0,)), ((), ())), precision=lax.Precision.HIGHEST
        )
        if step == 0:
            carried = contrib
        else:
            carried = passed_along(carried, "dp", 1) + contrib
    carried = passed_along(carried, "dp", 1 - STEPS)
    return (image_grad, carried)


def solution(mesh):
    return jax.shard_map(
        per_device,
        mesh=mesh,
        in_specs=(P("dp", None), P("dp", None), P(), P()),
        out_specs=(P("dp", None), P("dp", None)),
        check_vma=False,
    )
```

profile of v0, /device:TPU:1, one launch (start us, length us, event | category | flops | bytes accessed | tf_op | source)
XLA Modules:
  0.0 125.2 jit_solution(12653225909521346770)
XLA Ops:
  0.6 0.0 copy-start
  0.6 4.6 %collective-permute-start = (f32[256,1152]{1,0:T(8,128)}, f32[256,1152]{1,0:T(8,128)S(1)}, u32[]{:S(2)}, u32[]{:S(2)}) collective-permute-start(f32[256,1152]{1,0:T(8,128)} %param.5), channel_id=1, source_target_pairs={{0,1},{1,2},{2,3},{3,4},{4,5},{5,6},{6,7},{7,8},{8,9},{9,10},{10,1... | collective-permute-start | bytes 3538952 | tf_op jit(solution)/shard_map/ppermute | solution.py:11
  6.6 2.6 %fusion.25 = f32[256,256]{1,0:T(8,128)S(1)} fusion(f32[256,1152]{1,0:T(8,128)S(1)} %copy-done, f32[256,1152]{1,0:T(8,128)} %param.5, f32[]{:T(128)} %bitcast.26, f32[]{:T(128)} %bitcast), kind=kOutput, calls=%fused_computation.33 | convolution fusion | flops 906690560 | bytes 2621448 | tf_op jit(solution)/shard_map/dot_general | solution.py:17
  9.2 1.3 %fusion.27 = f32[256,1152]{1,0:T(8,128)S(1)} fusion(f32[256,256]{1,0:T(8,128)S(1)} %fusion.25, f32[256,1152]{1,0:T(8,128)S(1)} %copy-done), kind=kOutput, calls=%fused_computation.36 | convolution fusion | flops 905969664 | bytes 2621440 | tf_op jit(solution)/shard_map/dot_general | solution.py:40
  10.5 1.9 %collective-permute-start.3 = (f32[256,1152]{1,0:T(8,128)S(1)}, f32[256,1152]{1,0:T(8,128)S(1)}, u32[]{:S(2)}, u32[]{:S(2)}) collective-permute-start(f32[256,1152]{1,0:T(8,128)S(1)} %fusion.27), channel_id=1, source_target_pairs={{0,1},{1,2},{2,3},{3,4},{4,5},{5,6},{6,7},{7,8},{8,9},{9,10},{10,1... | collective-permute-start | bytes 3538952 | tf_op jit(solution)/shard_map/ppermute | solution.py:11
  12.4 6.3 %collective-permute-done = f32[256,1152]{1,0:T(8,128)S(1)} collective-permute-done((f32[256,1152]{1,0:T(8,128)}, f32[256,1152]{1,0:T(8,128)S(1)}, u32[]{:S(2)}, u32[]{:S(2)}) %collective-permute-start) | collective-permute-done | bytes 1179680 | tf_op jit(solution)/shard_map/ppermute | solution.py:11
  18.7 4.3 %collective-permute-start.1 = (f32[256,1152]{1,0:T(8,128)S(1)}, f32[256,1152]{1,0:T(8,128)S(1)}, u32[]{:S(2)}, u32[]{:S(2)}) collective-permute-start(f32[256,1152]{1,0:T(8,128)S(1)} %collective-permute-done), channel_id=1, source_target_pairs={{0,1},{1,2},{2,3},{3,4},{4,5},{5,6},{6,7},{7,8},{8,9},{9,10},{10,1... | collective-permute-start | bytes 3538952 | tf_op jit(solution)/shard_map/ppermute | solution.py:11
  23.0 1.3 %fusion.15 = f32[256,256]{1,0:T(8,128)S(1)} fusion(f32[256,1152]{1,0:T(8,128)S(1)} %copy-done, f32[256,1152]{1,0:T(8,128)S(1)} %collective-permute-done, f32[]{:T(128)} %bitcast.29, f32[]{:T(128)} %bitcast), kind=kOutput, calls=%fused_computation.23 | convolution fusion | flops 906362880 | bytes 2621448 | tf_op jit(solution)/shard_map/dot_general | solution.py:17
  24.3 7.0 %collective-permute-done.3 = f32[256,1152]{1,0:T(8,128)S(1)} collective-permute-done((f32[256,1152]{1,0:T(8,128)S(1)}, f32[256,1152]{1,0:T(8,128)S(1)}, u32[]{:S(2)}, u32[]{:S(2)}) %collective-permute-start.3) | collective-permute-done | bytes 1179680 | tf_op jit(solution)/shard_map/ppermute | solution.py:11
  31.3 1.3 %convolution_add_fusion = f32[256,1152]{1,0:T(8,128)S(1)} fusion(f32[256,1152]{1,0:T(8,128)S(1)} %collective-permute-done.3, f32[256,256]{1,0:T(8,128)S(1)} %fusion.15, f32[256,1152]{1,0:T(8,128)S(1)} %copy-done), kind=kOutput, calls=%fused_computation | convolution fusion | flops 906264576 | bytes 3801088 | tf_op jit(solution)/shard_map/dot_general | solution.py:40
  32.5 4.4 %collective-permute-start.4 = (f32[256,1152]{1,0:T(8,128)S(1)}, f32[256,1152]{1,0:T(8,128)S(1)}, u32[]{:S(2)}, u32[]{:S(2)}) collective-permute-start(f32[256,1152]{1,0:T(8,128)S(1)} %convolution_add_fusion), channel_id=1, source_target_pairs={{0,1},{1,2},{2,3},{3,4},{4,5},{5,6},{6,7},{7,8},{8,9},{9,10},{10,1... | collective-permute-start | bytes 3538952 | tf_op jit(solution)/shard_map/ppermute | solution.py:11
  36.9 7.0 %collective-permute-done.1 = f32[256,1152]{1,0:T(8,128)S(1)} collective-permute-done((f32[256,1152]{1,0:T(8,128)S(1)}, f32[256,1152]{1,0:T(8,128)S(1)}, u32[]{:S(2)}, u32[]{:S(2)}) %collective-permute-start.1) | collective-permute-done | bytes 1179680 | tf_op jit(solution)/shard_map/ppermute | solution.py:11
  43.9 4.4 %collective-permute-start.2 = (f32[256,1152]{1,0:T(8,128)S(1)}, f32[256,1152]{1,0:T(8,128)S(1)}, u32[]{:S(2)}, u32[]{:S(2)}) collective-permute-start(f32[256,1152]{1,0:T(8,128)S(1)} %collective-permute-done.1), channel_id=1, source_target_pairs={{0,1},{1,2},{2,3},{3,4},{4,5},{5,6},{6,7},{7,8},{8,9},{9,10},{10,1... | collective-permute-start | bytes 3538952 | tf_op jit(solution)/shard_map/ppermute | solution.py:11
  48.3 1.3 %fusion.18 = f32[256,256]{1,0:T(8,128)S(1)} fusion(f32[256,1152]{1,0:T(8,128)S(1)} %copy-done, f32[256,1152]{1,0:T(8,128)S(1)} %collective-permute-done.1, f32[]{:T(128)} %bitcast.28, f32[]{:T(128)} %bitcast), kind=kOutput, calls=%fused_computation.26 | convolution fusion | flops 906362880 | bytes 2621448 | tf_op jit(solution)/shard_map/dot_general | solution.py:17
  49.6 1.3 %fusion.28 = f32[256,1152]{1,0:T(8,128)S(1)} fusion(f32[256,256]{1,0:T(8,128)S(1)} %fusion.18, f32[256,1152]{1,0:T(8,128)S(1)} %copy-done), kind=kOutput, calls=%fused_computation.37 | convolution fusion | flops 905969664 | bytes 2621440 | tf_op jit(solution)/shard_map/dot_general | solution.py:40
  50.9 5.7 %collective-permute-done.4 = f32[256,1152]{1,0:T(8,128)S(1)} collective-permute-done((f32[256,1152]{1,0:T(8,128)S(1)}, f32[256,1152]{1,0:T(8,128)S(1)}, u32[]{:S(2)}, u32[]{:S(2)}) %collective-permute-start.4) | collective-permute-done | bytes 1179680 | tf_op jit(solution)/shard_map/ppermute | solution.py:11
  56.6 0.1 add.61
  56.7 4.4 %collective-permute-start.5 = (f32[256,1152]{1,0:T(8,128)S(1)}, f32[256,1152]{1,0:T(8,128)S(1)}, u32[]{:S(2)}, u32[]{:S(2)}) collective-permute-start(f32[256,1152]{1,0:T(8,128)S(1)} %add.61), channel_id=1, source_target_pairs={{0,1},{1,2},{2,3},{3,4},{4,5},{5,6},{6,7},{7,8},{8,9},{9,10},{10,1... | collective-permute-start | bytes 3538952 | tf_op jit(solution)/shard_map/ppermute | solution.py:11
  61.1 8.1 %collective-permute-done.2 = f32[256,1152]{1,0:T(8,128)S(1)} collective-permute-done((f32[256,1152]{1,0:T(8,128)S(1)}, f32[256,1152]{1,0:T(8,128)S(1)}, u32[]{:S(2)}, u32[]{:S(2)}) %collective-permute-start.2) | collective-permute-done | bytes 1179680 | tf_op jit(solution)/shard_map/ppermute | solution.py:11
  69.2 1.3 %fusion.21 = f32[256,256]{1,0:T(8,128)S(1)} fusion(f32[256,1152]{1,0:T(8,128)S(1)} %copy-done, f32[256,1152]{1,0:T(8,128)S(1)} %collective-permute-done.2, f32[]{:T(128)} %bitcast.27, f32[]{:T(128)} %bitcast), kind=kOutput, calls=%fused_computation.29 | convolution fusion | flops 906362880 | bytes 2621448 | tf_op jit(solution)/shard_map/dot_general | solution.py:17
  70.5 1.3 %fusion.29 = f32[256,1152]{1,0:T(8,128)S(1)} fusion(f32[256,256]{1,0:T(8,128)S(1)} %fusion.21, f32[256,1152]{1,0:T(8,128)S(1)} %copy-done), kind=kOutput, calls=%fused_computation.38 | convolution fusion | flops 905969664 | bytes 2621440 | tf_op jit(solution)/shard_map/dot_general | solution.py:40
  71.8 0.0 copy-start.1
  71.8 10.1 %collective-permute-done.5 = f32[256,1152]{1,0:T(8,128)S(1)} collective-permute-done((f32[256,1152]{1,0:T(8,128)S(1)}, f32[256,1152]{1,0:T(8,128)S(1)}, u32[]{:S(2)}, u32[]{:S(2)}) %collective-permute-start.5) | collective-permute-done | bytes 1179680 | tf_op jit(solution)/shard_map/ppermute | solution.py:11
  81.8 0.1 add.62
  82.0 17.2 %collective-permute-start.6 = (f32[256,1152]{1,0:T(8,128)S(1)}, f32[256,1152]{1,0:T(8,128)S(1)}, u32[]{:S(2)}, u32[]{:S(2)}) collective-permute-start(f32[256,1152]{1,0:T(8,128)S(1)} %add.62), channel_id=1, source_target_pairs={{0,509},{1,510},{2,511},{3,0},{4,1},{5,2},{6,3},{7,4},{8,5},{9,6},... | collective-permute-start | bytes 3538952 | tf_op jit(solution)/shard_map/ppermute | solution.py:11
  99.2 0.0 copy-done.1
  99.2 1.2 fusion.26
  100.4 1.2 convolution_add_fusion.3
  101.7 1.2 convolution_add_fusion.2
  102.9 2.3 %convolution_add_fusion.1 = f32[256,1152]{1,0:T(8,128)} fusion(f32[256,1152]{1,0:T(8,128)S(1)} %convolution_add_fusion.2, f32[256,256]{1,0:T(8,128)S(1)} %fusion.21, f32[256,1152]{1,0:T(8,128)S(1)} %collective-permute-done.2), kind=kOutput, calls=%fused_computation.1 | convolution fusion | flops 906264576 | bytes 3801088 | tf_op jit(solution)/shard_map/dot_general | solution.py:39
  105.2 19.0 %collective-permute-done.6 = f32[256,1152]{1,0:T(8,128)S(1)} collective-permute-done((f32[256,1152]{1,0:T(8,128)S(1)}, f32[256,1152]{1,0:T(8,128)S(1)}, u32[]{:S(2)}, u32[]{:S(2)}) %collective-permute-start.6) | collective-permute-done | bytes 1179680 | tf_op jit(solution)/shard_map/ppermute | solution.py:11
  124.2 1.0 copy.9
  (1 shorter events, 0.0 us)
Async XLA Ops:
  0.6 6.0 %copy-start = (f32[256,1152]{1,0:T(8,128)S(1)}, f32[256,1152]{1,0:T(8,128)}, u32[]{:S(2)}) copy-start(f32[256,1152]{1,0:T(8,128)} %param.4) | copy-start | bytes 3538948
  0.6 18.1 %collective-permute-start = (f32[256,1152]{1,0:T(8,128)}, f32[256,1152]{1,0:T(8,128)S(1)}, u32[]{:S(2)}, u32[]{:S(2)}) collective-permute-start(f32[256,1152]{1,0:T(8,128)} %param.5), channel_id=1, source_target_pairs={{0,1},{1,2},{2,3},{3,4},{4,5},{5,6},{6,7},{7,8},{8,9},{9,10},{10,1... | collective-permute-start | bytes 3538952 | tf_op jit(solution)/shard_map/ppermute | solution.py:11
  10.5 20.8 %collective-permute-start.3 = (f32[256,1152]{1,0:T(8,128)S(1)}, f32[256,1152]{1,0:T(8,128)S(1)}, u32[]{:S(2)}, u32[]{:S(2)}) collective-permute-start(f32[256,1152]{1,0:T(8,128)S(1)} %fusion.27), channel_id=1, source_target_pairs={{0,1},{1,2},{2,3},{3,4},{4,5},{5,6},{6,7},{7,8},{8,9},{9,10},{10,1... | collective-permute-start | bytes 3538952 | tf_op jit(solution)/shard_map/ppermute | solution.py:11
  18.7 25.2 %collective-permute-start.1 = (f32[256,1152]{1,0:T(8,128)S(1)}, f32[256,1152]{1,0:T(8,128)S(1)}, u32[]{:S(2)}, u32[]{:S(2)}) collective-permute-start(f32[256,1152]{1,0:T(8,128)S(1)} %collective-permute-done), channel_id=1, source_target_pairs={{0,1},{1,2},{2,3},{3,4},{4,5},{5,6},{6,7},{7,8},{8,9},{9,10},{10,1... | collective-permute-start | bytes 3538952 | tf_op jit(solution)/shard_map/ppermute | solution.py:11
  32.5 24.0 %collective-permute-start.4 = (f32[256,1152]{1,0:T(8,128)S(1)}, f32[256,1152]{1,0:T(8,128)S(1)}, u32[]{:S(2)}, u32[]{:S(2)}) collective-permute-start(f32[256,1152]{1,0:T(8,128)S(1)} %convolution_add_fusion), channel_id=1, source_target_pairs={{0,1},{1,2},{2,3},{3,4},{4,5},{5,6},{6,7},{7,8},{8,9},{9,10},{10,1... | collective-permute-start | bytes 3538952 | tf_op jit(solution)/shard_map/ppermute | solution.py:11
  43.9 25.3 %collective-permute-start.2 = (f32[256,1152]{1,0:T(8,128)S(1)}, f32[256,1152]{1,0:T(8,128)S(1)}, u32[]{:S(2)}, u32[]{:S(2)}) collective-permute-start(f32[256,1152]{1,0:T(8,128)S(1)} %collective-permute-done.1), channel_id=1, source_target_pairs={{0,1},{1,2},{2,3},{3,4},{4,5},{5,6},{6,7},{7,8},{8,9},{9,10},{10,1... | collective-permute-start | bytes 3538952 | tf_op jit(solution)/shard_map/ppermute | solution.py:11
  56.7 25.2 %collective-permute-start.5 = (f32[256,1152]{1,0:T(8,128)S(1)}, f32[256,1152]{1,0:T(8,128)S(1)}, u32[]{:S(2)}, u32[]{:S(2)}) collective-permute-start(f32[256,1152]{1,0:T(8,128)S(1)} %add.61), channel_id=1, source_target_pairs={{0,1},{1,2},{2,3},{3,4},{4,5},{5,6},{6,7},{7,8},{8,9},{9,10},{10,1... | collective-permute-start | bytes 3538952 | tf_op jit(solution)/shard_map/ppermute | solution.py:11
  71.8 27.4 %copy-start.1 = (f32[256,1152]{1,0:T(8,128)S(1)}, f32[256,1152]{1,0:T(8,128)}, u32[]{:S(2)}) copy-start(f32[256,1152]{1,0:T(8,128)} %param.5) | copy-start | bytes 3538948
  82.0 42.2 %collective-permute-start.6 = (f32[256,1152]{1,0:T(8,128)S(1)}, f32[256,1152]{1,0:T(8,128)S(1)}, u32[]{:S(2)}, u32[]{:S(2)}) collective-permute-start(f32[256,1152]{1,0:T(8,128)S(1)} %add.62), channel_id=1, source_target_pairs={{0,509},{1,510},{2,511},{3,0},{4,1},{5,2},{6,3},{7,4},{8,5},{9,6},... | collective-permute-start | bytes 3538952 | tf_op jit(solution)/shard_map/ppermute | solution.py:11
where the time goes:
time: 126 us; the launch traced here: 125 us
  waiting for transfers between devices  63.1 us (50%)
  starting transfers between devices  41.2 us (33%)
  matrix products  17.5 us (14%)
  between operations  2.14 us (2%)
    ppermute x7, waiting for transfers between devices, passed_along(): lax.ppermute(shard, axis, [(i, (i + by) % peers) for i in range(peers)])  63.1 us
    ppermute x7, starting transfers between devices, passed_along(): lax.ppermute(shard, axis, [(i, (i + by) % peers) for i in range(peers)])  41.2 us
    dot_general x4, matrix products, pair_grads(): lax.dot_general(images, visit, (((1,), (1,)), ((), ())), precision=lax.Pr...  6.37 us
    dot_general x4, matrix products, per_device(): jnp.dot(grads, visit, precision=lax.Precision.HIGHEST)  6 us
    dot_general x4, matrix products, per_device(): lax.dot_general(grads, images, (((0,), (0,)), ((), ())), precision=lax.Pr...  5.1 us
  transfers between devices with their start and end apart: 7, of which 7 were waited for; matrix products, arithmetic and copies ran while one was open for 14% of the time, Pallas kernels for 0%

commit v1 on v0

v1 whole, which is shorter than its diff:
```python
import functools

import jax
import jax.numpy as jnp
from jax import lax
from jax.experimental import pallas as pl
from jax.experimental.pallas import tpu as pltpu
from jax.sharding import PartitionSpec as P

MESH = pl.DeviceIdType.MESH
CHUNKS = 4
SIB, D1, D2, D3, E2, E3 = range(6)
NT = (((1,), (1,)), ((), ()))


def halves(value):
    high = value.astype(jnp.bfloat16)
    return high, (value - high.astype(jnp.float32)).astype(jnp.bfloat16)


def product(a, b, dims=(((1,), (0,)), ((), ()))):
    (ah, al), (bh, bl) = a, b

    def dot(u, v):
        return lax.dot_general(u, v, dims, preferred_element_type=jnp.float32)

    return dot(ah, bh) + (dot(ah, bl) + dot(al, bh))


def kernel(n, x_ref, y_ref, ls_ref, bias_ref, xg_ref, yg_ref, own, high, low, held, acc, scale, load_sem, out_sem, send_sem, recv_sem, left_sem):
    me = lax.axis_index("dp")
    core = lax.rem(me, 2)
    sib = me + 1 - 2 * core
    right, left = lax.rem(me + 2, n), lax.rem(me + n - 2, n)
    front, back = lax.rem(me + n - 2 + 4 * core, n), lax.rem(me + n + 2 - 4 * core, n)
    rows = own.shape[1]
    part = rows // CHUNKS

    barrier = pltpu.get_barrier_semaphore()
    for peer in (left, sib):
        pl.semaphore_signal(barrier, inc=1, device_id=(peer,), device_id_type=MESH)

    def load(slot, ref):
        return pltpu.make_async_copy(ref, own.at[slot], load_sem.at[slot])

    @pl.when(core == 0)
    def _():
        load(0, x_ref).start()
        load(1, y_ref).start()

    @pl.when(core == 1)
    def _():
        load(0, y_ref).start()
        load(1, x_ref).start()

    def send(src, slot, chunk, peer):
        at = pl.ds(chunk * part, part)
        return pltpu.make_async_remote_copy(
            src_ref=src.at[at],
            dst_ref=held.at[slot, at],
            send_sem=send_sem.at[slot, chunk],
            recv_sem=recv_sem.at[slot, chunk],
            device_id=(peer,),
            device_id_type=MESH,
        )

    def send_a(chunk):
        return send(own.at[0], E2, chunk, front)

    def send_b(chunk):
        return send(own.at[1], D2, chunk, back)

    def send_sib(chunk):
        return send(own.at[1], SIB, chunk, sib)

    def pass_e2(chunk):
        return send(held.at[E2], D1, chunk, sib)

    def pass_d2(chunk):
        return send(held.at[D2], E3, chunk, sib)

    def relay_d1(chunk):
        return send(held.at[D1], D3, chunk, back)

    def start(which):
        for chunk in range(CHUNKS):
            which(chunk).start()

    load(0, x_ref).wait()
    load(1, y_ref).wait()
    pl.semaphore_wait(barrier, 2)
    pl.semaphore_signal(left_sem, inc=1, device_id=(right,), device_id_type=MESH)

    @pl.when(core == 0)
    def _():
        start(send_b)
        pl.semaphore_wait(left_sem, 1)
        start(send_a)

    @pl.when(core == 1)
    def _():
        start(send_a)
        pl.semaphore_wait(left_sem, 1)
        start(send_b)

    start(send_sib)

    scale[...] = jnp.exp(jnp.full(scale.shape, ls_ref[0], jnp.float32))
    offset = bias_ref[0]
    for slot in range(2):
        high[slot], low[slot] = halves(own[slot])

    def add_pairs(mine, other, count, first=False):
        theirs = halves(other)
        times = scale[:, :count]
        logits = product((high[mine], low[mine]), theirs, NT) * times + offset
        if first:
            shape = (rows, count)
            diag = lax.broadcasted_iota(jnp.int32, shape, 0) == lax.broadcasted_iota(jnp.int32, shape, 1)
            grads = jnp.where(diag, -times, times) / (1.0 + jnp.exp(jnp.where(diag, logits, -logits)))
        else:
            grads = times / (1.0 + jnp.exp(-logits))
        term = product(halves(grads), theirs)
        if first:
            acc[mine] = term
        else:
            acc[mine] += term

    add_pairs(0, own[1], rows, True)
    add_pairs(1, own[0], rows, True)
    for chunk in range(CHUNKS):
        send_sib(chunk).wait_recv()
    add_pairs(1, held[SIB], rows)

    half = CHUNKS // 2
    for chunk in range(CHUNKS):
        pass_slots = ((send_a, pass_e2), (send_b, pass_d2), (pass_e2, relay_d1))
        for arrives, leaves in pass_slots:
            arrives(chunk).wait_recv()
            leaves(chunk).start()
        if chunk % half == half - 1:
            for c in range(chunk + 1 - half, chunk + 1):
                pass_d2(c).wait_recv()
            at = pl.ds((chunk + 1 - half) * part, half * part)
            for mine, slot in ((1, E2), (1, E3), (0, D1), (0, D2)):
                add_pairs(mine, held[slot, at], half * part)

    def store(slot, ref):
        return pltpu.make_async_copy(acc.at[slot], ref, out_sem.at[slot])

    @pl.when(core == 0)
    def _():
        store(1, yg_ref).start()

    @pl.when(core == 1)
    def _():
        store(1, xg_ref).start()

    for chunk in range(CHUNKS):
        relay_d1(chunk).wait_recv()
        add_pairs(0, held[D3, pl.ds(chunk * part, part)], part)

    @pl.when(core == 0)
    def _():
        store(0, xg_ref).start()

    @pl.when(core == 1)
    def _():
        store(0, yg_ref).start()

    for which in (send_a, send_b, send_sib, pass_e2, pass_d2, relay_d1):
        for chunk in range(CHUNKS):
            which(chunk).wait_send()
    store(0, xg_ref).wait()
    store(1, yg_ref).wait()


def per_device(n, images, texts, log_scale, bias):
    rows, width = images.shape
    block = (rows, width)
    return pl.pallas_call(
        functools.partial(kernel, n),
        out_shape=(jax.ShapeDtypeStruct(block, jnp.float32),) * 2,
        in_specs=[pl.BlockSpec(memory_space=pl.ANY)] * 2 + [pl.BlockSpec(memory_space=pltpu.SMEM)] * 2,
        out_specs=(pl.BlockSpec(memory_space=pl.ANY),) * 2,
        scratch_shapes=[
            pltpu.VMEM((2, *block), jnp.float32),
            pltpu.VMEM((2, *block), jnp.bfloat16),
            pltpu.VMEM((2, *block), jnp.bfloat16),
            pltpu.VMEM((6, *block), jnp.float32),
            pltpu.VMEM((2, *block), jnp.float32),
            pltpu.VMEM((1, rows), jnp.float32),
            pltpu.SemaphoreType.DMA((2,)),
            pltpu.SemaphoreType.DMA((2,)),
            pltpu.SemaphoreType.DMA((6, CHUNKS)),
            pltpu.SemaphoreType.DMA((6, CHUNKS)),
            pltpu.SemaphoreType.REGULAR,
        ],
        compiler_params=pltpu.CompilerParams(collective_id=0, has_side_effects=True, vmem_limit_bytes=56 * 2**20),
    )(images, texts, log_scale, bias)


def solution(mesh):
    return jax.shard_map(
        functools.partial(per_device, mesh.shape["dp"]),
        mesh=mesh,
        in_specs=(P("dp", None), P("dp", None), P(), P()),
        out_specs=(P("dp", None), P("dp", None)),
        check_vma=False,
    )
```

time: 126 us -> 64.7 us (0.51)
  waiting for transfers between devices: 63.1 us -> 0 us
  Pallas kernels: 0 us -> 59 us
  starting transfers between devices: 41.2 us -> 0 us
  matrix products: 17.5 us -> 0 us
  local copies, waits for them, and re-layouts: 1.03 us -> 3.47 us
    ppermute x7 -> x0, waiting for transfers between devices: 63.1 us -> none  [passed_along(): lax.ppermute(shard, axis, [(i, (i + by) % peers) for i in range(peers)])]
    pallas_call x0 -> x1, Pallas kernels: none -> 59 us  [per_device(): pl.pallas_call(functools.partial(kernel, n), out_shape=(jax.ShapeDtypeStr...]
    ppermute x7 -> x0, starting transfers between devices: 41.2 us -> none  [passed_along(): lax.ppermute(shard, axis, [(i, (i + by) % peers) for i in range(peers)])]
    dot_general x12 -> x0, matrix products: 17.5 us -> none  [the longest x4 6.37 us: pair_grads(): lax.dot_general(images, visit, (((1,), (1,)), ((), ())), precision=lax.Pr...]
    unnamed x5 -> x4, local copies, waits for them, and re-layouts: 1.03 us -> 3.47 us
  transfers between devices with their start and end apart: 7 -> 0, of which waited for: 7 -> 0; matrix products, arithmetic and copies ran while one was open for 14% -> 0% of each run, Pallas kernels for 0% -> 0%
where the time goes in v1:
time: 64.7 us; the launch traced here: 64.5 us
  Pallas kernels  59 us (91%)
  local copies, waits for them, and re-layouts  3.47 us (5%)
  between operations  1.94 us (3%)
    pallas_call x1, Pallas kernels, per_device(): pl.pallas_call(functools.partial(kernel, n), out_shape=(jax.ShapeDtypeStr...  59 us
    unnamed x4, local copies, waits for them, and re-layouts  3.47 us

profile of v1, /device:TPU:1, one launch (start us, length us, event | category | flops | bytes accessed | tf_op | source)
XLA Modules:
  0.0 64.5 jit_solution(17505732894671828121)
XLA Ops:
  1.9 59.0 %shard_map.59 = (f32[256,1152]{1,0:T(8,128)}, f32[256,1152]{1,0:T(8,128)}) custom-call(f32[256,1152]{1,0:T(8,128)} %x_ref.1, f32[256,1152]{1,0:T(8,128)} %y_ref.1, f32[1]{0:T(128)S(6)} %copy.8.ls_ref, f32[1]{0:T(128)S(6)} %copy.9.bias_ref), custom_call_target="tpu_custom_call" | custom-call | tf_op jit(solution)/shard_map/pallas_call | solution.py:181
  61.0 0.0 copy-start
  61.0 2.5 %copy.10 = f32[256,1152]{1,0:T(8,128)} copy(f32[256,1152]{1,0:T(8,128)} %get-tuple-element.4) | data formatting | bytes 2359296
  63.4 0.0 copy-done
  63.4 1.0 %copy.11 = f32[256,1152]{1,0:T(8,128)} copy(f32[256,1152]{1,0:T(8,128)S(1)} %copy-done) | data formatting | bytes 2359296
Async XLA Ops:
  61.0 2.5 %copy-start = (f32[256,1152]{1,0:T(8,128)S(1)}, f32[256,1152]{1,0:T(8,128)}, u32[]{:S(2)}) copy-start(f32[256,1152]{1,0:T(8,128)} %get-tuple-element.5) | copy-start | bytes 3538948

commit v2 on v1

v2 whole, which is shorter than its diff:
```python
import functools

import jax
import jax.numpy as jnp
from jax import lax
from jax.experimental import pallas as pl
from jax.experimental.pallas import tpu as pltpu
from jax.sharding import PartitionSpec as P

MESH = pl.DeviceIdType.MESH
CHUNKS = 4
SIB, D1, D2, D3, E2, E3 = range(6)
HALVES = ((0, range(0, 2)), (2, range(2, 4)))
TAIL = (range(0, 2), range(2, 3), range(3, 4))
NT = (((1,), (1,)), ((), ()))


def halves(value):
    high = value.astype(jnp.bfloat16)
    return high, (value - high.astype(jnp.float32)).astype(jnp.bfloat16)


def dot(a, b, dims=(((1,), (0,)), ((), ()))):
    return lax.dot_general(a, b, dims, preferred_element_type=jnp.float32)


def kernel(n, x_ref, y_ref, ls_ref, bias_ref, a_acc, b_acc, own, high, low, held, stack, scale, load_sem, send_sem, recv_sem, left_sem):
    me = lax.axis_index("dp")
    core, chip = lax.rem(me, 2), lax.div(me, 2)
    sib = me + 1 - 2 * core
    right, left = lax.rem(me + 2, n), lax.rem(me + n - 2, n)
    front, back = lax.rem(me + n - 2 + 4 * core, n), lax.rem(me + n + 2 - 4 * core, n)
    rows = own.shape[1]
    part, half = rows // CHUNKS, rows // 2
    first, last = chip == 0, chip == n // 2 - 1

    barrier = pltpu.get_barrier_semaphore()

    def greet(peer):
        pl.semaphore_signal(barrier, inc=1, device_id=(peer,), device_id_type=MESH)

    greet(sib)
    greet(left)
    pl.when(jnp.logical_not(last))(lambda: greet(right))

    def load(slot, ref):
        return pltpu.make_async_copy(ref, own.at[slot], load_sem.at[slot])

    @pl.when(core == 0)
    def _():
        load(0, x_ref).start()
        load(1, y_ref).start()

    @pl.when(core == 1)
    def _():
        load(0, y_ref).start()
        load(1, x_ref).start()

    def send(src, slot, chunk, peer):
        at = pl.ds(chunk * part, part)
        return pltpu.make_async_remote_copy(
            src_ref=src.at[at],
            dst_ref=held.at[slot, at],
            send_sem=send_sem.at[slot, chunk],
            recv_sem=recv_sem.at[slot, chunk],
            device_id=(peer,),
            device_id_type=MESH,
        )

    def send_a(chunk):
        return send(own.at[0], E2, chunk, front)

    def send_b(chunk):
        return send(own.at[1], D2, chunk, back)

    def send_sib(chunk):
        return send(own.at[1], SIB, chunk, sib)

    def pass_e2(chunk):
        return send(held.at[E2], D1, chunk, sib)

    def pass_d2(chunk):
        return send(held.at[D2], E3, chunk, sib)

    def relay_d1(chunk):
        return send(held.at[D1], D3, chunk, back)

    def start(which):
        for chunk in range(CHUNKS):
            which(chunk).start()

    def arrive(which, chunks=range(CHUNKS)):
        for chunk in chunks:
            which(chunk).wait_recv()

    load(0, x_ref).wait()
    load(1, y_ref).wait()
    pl.semaphore_wait(barrier, jnp.where(first, 2, 3))
    pl.when(last)(lambda: pl.semaphore_signal(left_sem, inc=1, device_id=(right,), device_id_type=MESH))

    def start_right():
        pl.when(core == 0)(lambda: start(send_b))
        pl.when(core == 1)(lambda: start(send_a))

    def start_left():
        pl.when(core == 0)(lambda: start(send_a))
        pl.when(core == 1)(lambda: start(send_b))

    start_right()
    pl.when(jnp.logical_not(first))(start_left)
    start(send_sib)

    scale[...] = jnp.exp(jnp.full(scale.shape, ls_ref[0], jnp.float32))
    offset = bias_ref[0]
    for slot in range(2):
        high[slot], low[slot] = halves(own[slot])

    def add_pairs(mine, block, at, count, same=False):
        acc = (a_acc, b_acc)[mine]
        oh, ol = halves(block[pl.ds(at, count)])
        stack[:count], stack[count : 2 * count], stack[2 * count : 3 * count] = oh, ol, oh
        times = scale[:, :count]
        wide = dot(high[mine], stack[: 2 * count], NT)
        logits = (wide[:, :count] + (wide[:, count:] + dot(low[mine], oh, NT))) * times + offset
        if same:
            shape = (rows, count)
            diag = lax.broadcasted_iota(jnp.int32, shape, 0) == lax.broadcasted_iota(jnp.int32, shape, 1) + at
            grads = jnp.where(diag, -times, times) / (1.0 + jnp.exp(jnp.where(diag, logits, -logits)))
        else:
            grads = times / (1.0 + jnp.exp(-logits))
        gh, gl = halves(grads)
        term = dot(jnp.concatenate([gh, gh, gl], axis=1), stack[: 3 * count])
        if same and at == 0:
            acc[...] = term
        else:
            acc[...] += term

    for at in (0, half):
        add_pairs(0, own.at[1], at, half, True)
        add_pairs(1, own.at[0], at, half, True)
    for at, chunks in HALVES:
        arrive(send_sib, chunks)
        add_pairs(1, held.at[SIB], at * part, half)

    def add_e(at, chunks):
        add_pairs(1, held.at[E2], at * part, half)
        arrive(pass_d2, chunks)
        add_pairs(1, held.at[E3], at * part, half)

    def add_d(at):
        add_pairs(0, held.at[D1], at * part, half)
        add_pairs(0, held.at[D2], at * part, half)

    def take_e(chunk):
        send_a(chunk).wait_recv()
        pass_e2(chunk).start()

    def take_d(chunk):
        send_b(chunk).wait_recv()
        pass_d2(chunk).start()

    def take_d1(chunk):
        pass_e2(chunk).wait_recv()
        relay_d1(chunk).start()

    def add_d3(chunks):
        arrive(relay_d1, chunks)
        add_pairs(0, held.at[D3], chunks[0] * part, len(chunks) * part)

    @pl.when(jnp.logical_not(first))
    def _():
        for at, chunks in HALVES:
            for chunk in chunks:
                take_e(chunk)
                take_d(chunk)
                take_d1(chunk)
            add_e(at, chunks)
            add_d(at)
        for chunks in TAIL:
            add_d3(chunks)

    @pl.when(first)
    def _():
        pl.semaphore_wait(left_sem, 1)
        start_left()

    @pl.when(jnp.logical_and(first, core == 0))
    def _():
        for at, chunks in HALVES:
            for chunk in chunks:
                take_e(chunk)
            add_e(at, chunks)
        for at, chunks in HALVES:
            for chunk in chunks:
                take_d(chunk)
                take_d1(chunk)
            add_d(at)
        for chunks in TAIL:
            add_d3(chunks)

    @pl.when(jnp.logical_and(first, core == 1))
    def _():
        for at, chunks in HALVES:
            for chunk in chunks:
                take_d(chunk)
                take_d1(chunk)
            add_d(at)
        for (at, chunks), tail in zip(HALVES, TAIL):
            for chunk in chunks:
                take_e(chunk)
            add_d3(tail)
            add_e(at, chunks)
        for chunks in TAIL[2:]:
            add_d3(chunks)

    for which in (send_a, send_b, send_sib, pass_e2, pass_d2, relay_d1):
        for chunk in range(CHUNKS):
            which(chunk).wait_send()


def place(a_ref, b_ref, xg_ref, yg_ref, sem):
    core = lax.rem(lax.axis_index("dp"), 2)

    def put(slot, ref):
        return pltpu.make_async_copy((a_ref, b_ref)[slot], ref, sem.at[slot])

    @pl.when(core == 0)
    def _():
        put(0, xg_ref).start()
        put(1, yg_ref).start()

    @pl.when(core == 1)
    def _():
        put(0, yg_ref).start()
        put(1, xg_ref).start()

    put(0, xg_ref).wait()
    put(1, yg_ref).wait()


def per_device(n, images, texts, log_scale, bias):
    rows, width = images.shape
    block = (rows, width)
    hbm = [pltpu.with_memory_space_constraint(z, pltpu.HBM) for z in (images, texts)]
    grads = pl.pallas_call(
        functools.partial(kernel, n),
        out_shape=(pltpu.VMEM(block, jnp.float32),) * 2,
        in_specs=[pl.BlockSpec(memory_space=pl.ANY)] * 2 + [pl.BlockSpec(memory_space=pltpu.SMEM)] * 2,
        out_specs=(pl.BlockSpec(memory_space=pltpu.VMEM),) * 2,
        scratch_shapes=[
            pltpu.VMEM((2, *block), jnp.float32),
            pltpu.VMEM((2, *block), jnp.bfloat16),
            pltpu.VMEM((2, *block), jnp.bfloat16),
            pltpu.VMEM((6, *block), jnp.float32),
            pltpu.VMEM((3 * rows // 2, width), jnp.bfloat16),
            pltpu.VMEM((1, rows), jnp.float32),
            pltpu.SemaphoreType.DMA((2,)),
            pltpu.SemaphoreType.DMA((6, CHUNKS)),
            pltpu.SemaphoreType.DMA((6, CHUNKS)),
            pltpu.SemaphoreType.REGULAR,
        ],
        compiler_params=pltpu.CompilerParams(collective_id=0, has_side_effects=True, vmem_limit_bytes=40 * 2**20),
    )(*hbm, log_scale, bias)
    return pl.pallas_call(
        place,
        out_shape=(pltpu.HBM(block, jnp.float32),) * 2,
        in_specs=[pl.BlockSpec(memory_space=pl.ANY)] * 2,
        out_specs=(pl.BlockSpec(memory_space=pl.ANY),) * 2,
        scratch_shapes=[pltpu.SemaphoreType.DMA((2,))],
    )(*(pltpu.with_memory_space_constraint(z, pltpu.VMEM) for z in grads))


def solution(mesh):
    return jax.shard_map(
        functools.partial(per_device, mesh.shape["dp"]),
        mesh=mesh,
        in_specs=(P("dp", None), P("dp", None), P(), P()),
        out_specs=(P("dp", None), P("dp", None)),
        check_vma=False,
    )
```

time: 64.7 us -> 59.9 us (0.926)
  local copies, waits for them, and re-layouts: 3.47 us -> 0 us
  Pallas kernels: 59 us -> 57.4 us
    unnamed x4 -> x0, local copies, waits for them, and re-layouts: 3.47 us -> none
    pallas_call x1 -> x2, Pallas kernels: 59 us -> 57.4 us  [the longest x1 55.9 us: per_device(): pl.pallas_call(functools.partial(kernel, n), out_shape=(pltpu.VMEM(block,...]
where the time goes in v2:
time: 59.9 us; the launch traced here: 59.5 us
  Pallas kernels  57.4 us (96%)
  between operations  2.11 us (4%)
    pallas_call x1, Pallas kernels, per_device(): pl.pallas_call(functools.partial(kernel, n), out_shape=(pltpu.VMEM(block,...  55.9 us
    pallas_call x1, Pallas kernels, per_device(): pl.pallas_call(place, out_shape=(pltpu.HBM(block, jnp.float32),) * 2, in_...  1.43 us

profile of v2, /device:TPU:1, one launch (start us, length us, event | category | flops | bytes accessed | tf_op | source)
XLA Modules:
  0.0 59.5 jit_solution(5029140349418358828)
XLA Ops:
  1.9 55.9 %shard_map.59 = (f32[256,1152]{1,0:T(8,128)S(1)}, f32[256,1152]{1,0:T(8,128)S(1)}) custom-call(f32[256,1152]{1,0:T(8,128)} %x_ref.1, f32[256,1152]{1,0:T(8,128)} %y_ref.1, f32[1]{0:T(128)S(6)} %copy.6.ls_ref, f32[1]{0:T(128)S(6)} %copy.7.bias_ref), custom_call_target="tpu_custom_call" | custom-call | tf_op jit(solution)/shard_map/pallas_call | solution.py:245
  57.9 1.4 %shard_map.60 = (f32[256,1152]{1,0:T(8,128)}, f32[256,1152]{1,0:T(8,128)}) custom-call(f32[256,1152]{1,0:T(8,128)S(1)} %get-tuple-element.4.a_ref, f32[256,1152]{1,0:T(8,128)S(1)} %get-tuple-element.5.b_ref), custom_call_target="tpu_custom_call" | custom-call | tf_op jit(solution)/shard_map/pallas_call | solution.py:264

commit v3 on v0

v3 whole, which is shorter than its diff:
```python
import functools

import jax
import jax.numpy as jnp
from jax import lax
from jax.experimental import pallas as pl
from jax.experimental.pallas import tpu as pltpu
from jax.sharding import PartitionSpec as P

MESH = pl.DeviceIdType.MESH
A, B, SIB, D1, D2, D3, E2, E3 = range(8)
NT = (((1,), (1,)), ((), ()))
START = ((B, 0), (B, 1), (A, 0), (A, 1), (SIB, 0), (SIB, 1))
LOCAL = len(START)
USUAL = START + ((E2, 0), (D1, 0), (E2, 1), (D1, 1), (D2, 0), (E3, 0), (D2, 1), (E3, 1), (D3, 0), (D3, 1))
FIRST = (
    START + ((E2, 0), (D1, 0), (E2, 1), (D1, 1), (E3, 0), (E3, 1), (D2, 0), (D2, 1), (D3, 0), (D3, 1)),
    START + ((D1, 0), (E2, 0), (D1, 1), (E2, 1), (D2, 0), (D2, 1), (E3, 0), (D3, 0), (E3, 1), (D3, 1)),
)
LAST = (
    START + ((D1, 0), (D1, 1), (D2, 0), (E2, 0), (D2, 1), (E2, 1), (D3, 0), (E3, 0), (D3, 1), (E3, 1)),
    START + ((E2, 0), (E2, 1), (E3, 0), (D1, 0), (E3, 1), (D1, 1), (D2, 0), (D2, 1), (D3, 0), (D3, 1)),
)


def halves(value):
    high = value.astype(jnp.bfloat16)
    return high, (value - high.astype(jnp.float32)).astype(jnp.bfloat16)


def dot(a, b, dims=(((1,), (0,)), ((), ()))):
    return lax.dot_general(a, b, dims, preferred_element_type=jnp.float32)


def pick(index, values):
    result = values[0]
    for k in range(1, len(values)):
        if values[k] != values[k - 1]:
            result = jnp.where(index >= k, values[k], result)
    return result


def kernel(n, x_ref, y_ref, ls_ref, bias_ref, acc, pool, high, low, stack, scale, load_sem, send_sem, recv_sem, left_sem):
    me = lax.axis_index("dp")
    core, chip = lax.rem(me, 2), lax.div(me, 2)
    sib = me + 1 - 2 * core
    right, left = lax.rem(me + 2, n), lax.rem(me + n - 2, n)
    front, back = lax.rem(me + n - 2 + 4 * core, n), lax.rem(me + n + 2 - 4 * core, n)
    rows = pool.shape[1]
    half = rows // 2
    first, last = chip == 0, chip == n // 2 - 1

    barrier = pltpu.get_barrier_semaphore()

    def greet(peer):
        pl.semaphore_signal(barrier, inc=1, device_id=(peer,), device_id_type=MESH)

    greet(sib)
    greet(left)
    pl.when(jnp.logical_not(last))(lambda: greet(right))
    opens, early, closes = first & (core == 0), first & (core == 1), last & (core == 1)
    before, after = lax.rem(me + n - 1, n), lax.rem(me + 1, n)
    pl.when(opens)(lambda: greet(before))

    def load(slot, ref):
        return pltpu.make_async_copy(ref, pool.at[slot], load_sem.at[slot])

    @pl.when(core == 0)
    def _():
        load(A, x_ref).start()
        load(B, y_ref).start()

    @pl.when(core == 1)
    def _():
        load(A, y_ref).start()
        load(B, x_ref).start()

    def send(src, dst, h, peer, sem=None):
        at = pl.ds(h * half, half)
        return pltpu.make_async_remote_copy(
            src_ref=pool.at[src, at],
            dst_ref=pool.at[dst, at],
            send_sem=send_sem.at[dst if sem is None else sem, h],
            recv_sem=recv_sem.at[dst, h],
            device_id=(peer,),
            device_id_type=MESH,
        )

    def send_a(h):
        return send(A, E2, h, front)

    def send_b(h):
        return send(B, D2, h, back)

    def send_sib(h):
        return send(B, SIB, h, sib)

    def pass_e2(h):
        return send(E2, D1, h, sib)

    def pass_d2(h):
        return send(D2, E3, h, sib)

    def relay_d1(h):
        return send(D1, D3, h, back)

    def relay_e2(h):
        return send(E2, D3, h, before, A)

    def start(which):
        which(0).start()
        which(1).start()

    acc[...] = jnp.zeros_like(acc)
    scale[...] = jnp.exp(jnp.full(scale.shape, ls_ref[0], jnp.float32))
    offset = bias_ref[0]
    load(A, x_ref).wait()
    load(B, y_ref).wait()
    pl.semaphore_wait(barrier, jnp.where(first, 2, jnp.where(closes, 4, 3)))
    pl.when(last)(lambda: pl.semaphore_signal(left_sem, inc=1, device_id=(right,), device_id_type=MESH))
    pl.when(closes)(lambda: pl.semaphore_signal(left_sem, inc=1, device_id=(after,), device_id_type=MESH))
    pl.when(opens)(lambda: start(send_b))
    pl.when(jnp.logical_not(opens))(lambda: start(send_a))
    start(send_sib)
    for slot in range(2):
        high[slot], low[slot] = halves(pool[slot])

    def take_e2(h):
        send_a(h).wait_recv()
        pass_e2(h).start()
        pl.when(opens)(lambda: relay_e2(h).start())

    def take_d2(h):
        send_b(h).wait_recv()
        pass_d2(h).start()

    def take_d1(h):
        pass_e2(h).wait_recv()
        pl.when(jnp.logical_not(early))(lambda: relay_d1(h).start())

    def open_left():
        pl.when(early)(lambda: pl.semaphore_wait(left_sem, 1))
        pl.when(opens)(lambda: pl.semaphore_wait(left_sem, 2))
        pl.when(opens)(lambda: start(send_a))

    def start_later():
        pl.when(jnp.logical_not(opens))(lambda: start(send_b))

    def add_pairs(mine, slot, h):
        at = pl.multiple_of(h * half, half)
        oh, ol = halves(pool[slot, pl.ds(at, half)])
        stack[:half], stack[half : 2 * half], stack[2 * half :] = oh, ol, oh
        times = scale[...]
        wide = dot(high[mine], stack[: 2 * half], NT)
        logits = (wide[:, :half] + (wide[:, half:] + dot(low[mine], oh, NT))) * times + offset
        shape = (rows, half)
        gap = lax.broadcasted_iota(jnp.int32, shape, 0) - lax.broadcasted_iota(jnp.int32, shape, 1)
        positive = gap == jnp.where(slot <= B, at, rows)
        grads = jnp.where(positive, -times, times) / (1.0 + jnp.exp(jnp.where(positive, logits, -logits)))
        gh, gl = halves(grads)
        acc[mine] += dot(jnp.concatenate([gh, gh, gl], axis=1), stack[...])

    def by_place(usual, zero, one, last_zero, last_one):
        ends = jnp.where(first, jnp.where(core == 0, zero, one), jnp.where(core == 0, last_zero, last_one))
        return jnp.where(first | last, ends, usual)

    def step_of(block, h):
        return by_place(*(tasks.index((block, h)) for tasks in (USUAL, *FIRST, *LAST)))

    def recv(which, h):
        return lambda: which(h).wait_recv()

    events = [(jnp.int32(LOCAL), open_left), (jnp.where(first, LOCAL + 2, LOCAL), start_later)]
    for h in range(2):
        events += [
            (step_of(SIB, h), recv(send_sib, h)),
            (step_of(E2, h), functools.partial(take_e2, h)),
            (step_of(D2, h), functools.partial(take_d2, h)),
            (step_of(E3, h), recv(pass_d2, h)),
            (step_of(D1, h), functools.partial(take_d1, h)),
            (step_of(D3, h), recv(relay_d1, h)),
        ]

    def by_order(i, part):
        return [pick(i, [task[part] for task in tasks]) for tasks in (USUAL, *FIRST, *LAST)]

    def step(i, _):
        for at_step, event in events:
            pl.when(i == at_step)(event)
        slot, h = (by_place(*by_order(i, part)) for part in range(2))
        mine = jnp.where((slot == A) | (slot == SIB) | (slot >= E2), 1, 0)
        add_pairs(mine, slot, h)
        return 0

    lax.fori_loop(0, len(USUAL), step, 0)

    for h in range(2):
        for which in (send_a, send_b, send_sib, pass_e2, pass_d2):
            which(h).wait_send()
        pl.when(jnp.logical_not(early))(lambda: relay_d1(h).wait_send())
        pl.when(opens)(lambda: relay_e2(h).wait_send())


def place(acc, xg_ref, yg_ref, sem):
    core = lax.rem(lax.axis_index("dp"), 2)

    def put(slot, ref):
        return pltpu.make_async_copy(acc.at[slot], ref, sem.at[slot])

    @pl.when(core == 0)
    def _():
        put(0, xg_ref).start()
        put(1, yg_ref).start()

    @pl.when(core == 1)
    def _():
        put(0, yg_ref).start()
        put(1, xg_ref).start()

    put(0, xg_ref).wait()
    put(1, yg_ref).wait()


def per_device(n, images, texts, log_scale, bias):
    rows, width = images.shape
    block = (rows, width)
    hbm = [pltpu.with_memory_space_constraint(z, pltpu.HBM) for z in (images, texts)]
    grads = pl.pallas_call(
        functools.partial(kernel, n),
        out_shape=pltpu.VMEM((2, *block), jnp.float32),
        in_specs=[pl.BlockSpec(memory_space=pl.ANY)] * 2 + [pl.BlockSpec(memory_space=pltpu.SMEM)] * 2,
        out_specs=pl.BlockSpec(memory_space=pltpu.VMEM),
        scratch_shapes=[
            pltpu.VMEM((8, *block), jnp.float32),
            pltpu.VMEM((2, *block), jnp.bfloat16),
            pltpu.VMEM((2, *block), jnp.bfloat16),
            pltpu.VMEM((3 * rows // 2, width), jnp.bfloat16),
            pltpu.VMEM((1, rows // 2), jnp.float32),
            pltpu.SemaphoreType.DMA((2,)),
            pltpu.SemaphoreType.DMA((8, 2)),
            pltpu.SemaphoreType.DMA((8, 2)),
            pltpu.SemaphoreType.REGULAR,
        ],
        compiler_params=pltpu.CompilerParams(collective_id=0, has_side_effects=True, vmem_limit_bytes=40 * 2**20),
    )(*hbm, log_scale, bias)
    return pl.pallas_call(
        place,
        out_shape=(pltpu.HBM(block, jnp.float32),) * 2,
        in_specs=[pl.BlockSpec(memory_space=pl.ANY)],
        out_specs=(pl.BlockSpec(memory_space=pl.ANY),) * 2,
        scratch_shapes=[pltpu.SemaphoreType.DMA((2,))],
    )(pltpu.with_memory_space_constraint(grads, pltpu.VMEM))


def solution(mesh):
    return jax.shard_map(
        functools.partial(per_device, mesh.shape["dp"]),
        mesh=mesh,
        in_specs=(P("dp", None), P("dp", None), P(), P()),
        out_specs=(P("dp", None), P("dp", None)),
        check_vma=False,
    )
```

time: 126 us -> 55 us (0.44)
  waiting for transfers between devices: 63.1 us -> 0 us
  Pallas kernels: 0 us -> 52.9 us
  starting transfers between devices: 41.2 us -> 0 us
  matrix products: 17.5 us -> 0 us
    ppermute x7 -> x0, waiting for transfers between devices: 63.1 us -> none  [passed_along(): lax.ppermute(shard, axis, [(i, (i + by) % peers) for i in range(peers)])]
    pallas_call x0 -> x2, Pallas kernels: none -> 52.9 us  [the longest x1 51.5 us: per_device(): pl.pallas_call(functools.partial(kernel, n), out_shape=pltpu.VMEM((2, *bl...]
    ppermute x7 -> x0, starting transfers between devices: 41.2 us -> none  [passed_along(): lax.ppermute(shard, axis, [(i, (i + by) % peers) for i in range(peers)])]
    dot_general x12 -> x0, matrix products: 17.5 us -> none  [the longest x4 6.37 us: pair_grads(): lax.dot_general(images, visit, (((1,), (1,)), ((), ())), precision=lax.Pr...]
  transfers between devices with their start and end apart: 7 -> 0, of which waited for: 7 -> 0; matrix products, arithmetic and copies ran while one was open for 14% -> 0% of each run, Pallas kernels for 0% -> 0%
where the time goes in v3:
time: 55 us; the launch traced here: 54.8 us
  Pallas kernels  52.9 us (96%)
  between operations  1.93 us (4%)
    pallas_call x1, Pallas kernels, per_device(): pl.pallas_call(functools.partial(kernel, n), out_shape=pltpu.VMEM((2, *bl...  51.5 us
    pallas_call x1, Pallas kernels, per_device(): pl.pallas_call(place, out_shape=(pltpu.HBM(block, jnp.float32),) * 2, in_...  1.43 us

profile of v3, /device:TPU:1, one launch (start us, length us, event | category | flops | bytes accessed | tf_op | source)
XLA Modules:
  0.0 54.8 jit_solution(11967770826401326763)
XLA Ops:
  1.9 51.5 %shard_map.59.acc = f32[2,256,1152]{2,1,0:T(8,128)S(1)} custom-call(f32[256,1152]{1,0:T(8,128)} %x_ref.1, f32[256,1152]{1,0:T(8,128)} %y_ref.1, f32[1]{0:T(128)S(6)} %copy.6.ls_ref, f32[1]{0:T(128)S(6)} %copy.7.bias_ref), custom_call_target="tpu_custom_call" | custom-call | tf_op jit(solution)/shard_map/pallas_call | solution.py:228
  53.4 1.4 %shard_map.60 = (f32[256,1152]{1,0:T(8,128)}, f32[256,1152]{1,0:T(8,128)}) custom-call(f32[2,256,1152]{2,1,0:T(8,128)S(1)} %shard_map.59.acc), custom_call_target="tpu_custom_call" | custom-call | tf_op jit(solution)/shard_map/pallas_call | solution.py:246

commit v4 on v3

--- a/solution.py
+++ b/solution.py
@@ -12,14 +12,14 @@
 NT = (((1,), (1,)), ((), ()))
 START = ((B, 0), (B, 1), (A, 0), (A, 1), (SIB, 0), (SIB, 1))
 LOCAL = len(START)
-USUAL = START + ((E2, 0), (D1, 0), (E2, 1), (D1, 1), (D2, 0), (E3, 0), (D2, 1), (E3, 1), (D3, 0), (D3, 1))
+USUAL = START + ((E2, 0), (D2, 0), (D1, 0), (E3, 0), (E2, 1), (D2, 1), (D1, 1), (E3, 1), (D3, 0), (D3, 1))
 FIRST = (
-    START + ((E2, 0), (D1, 0), (E2, 1), (D1, 1), (E3, 0), (E3, 1), (D2, 0), (D2, 1), (D3, 0), (D3, 1)),
-    START + ((D1, 0), (E2, 0), (D1, 1), (E2, 1), (D2, 0), (D2, 1), (E3, 0), (D3, 0), (E3, 1), (D3, 1)),
+    START + ((E3, 0), (E2, 0), (D1, 0), (E3, 1), (E2, 1), (D1, 1), (D2, 0), (D2, 1), (D3, 0), (D3, 1)),
+    START + ((D2, 0), (D1, 0), (E2, 0), (D2, 1), (E2, 1), (D1, 1), (E3, 0), (D3, 0), (E3, 1), (D3, 1)),
 )
 LAST = (
-    START + ((D1, 0), (D1, 1), (D2, 0), (E2, 0), (D2, 1), (E2, 1), (D3, 0), (E3, 0), (D3, 1), (E3, 1)),
-    START + ((E2, 0), (E2, 1), (E3, 0), (D1, 0), (E3, 1), (D1, 1), (D2, 0), (D2, 1), (D3, 0), (D3, 1)),
+    USUAL,
+    START + ((E2, 0), (D1, 0), (E3, 0), (D2, 0), (E2, 1), (D1, 1), (E3, 1), (D2, 1), (D3, 0), (D3, 1)),
 )
 
 
@@ -55,12 +55,12 @@
     def greet(peer):
         pl.semaphore_signal(barrier, inc=1, device_id=(peer,), device_id_type=MESH)
 
+    cross = lax.rem(me + n - 1 + 2 * core, n)
+    opens, early, closes = first & (core == 0), first & (core == 1), last & (core == 1)
     greet(sib)
     greet(left)
     pl.when(jnp.logical_not(last))(lambda: greet(right))
-    opens, early, closes = first & (core == 0), first & (core == 1), last & (core == 1)
-    before, after = lax.rem(me + n - 1, n), lax.rem(me + 1, n)
-    pl.when(opens)(lambda: greet(before))
+    pl.when(jnp.logical_not(closes))(lambda: greet(cross))
 
     def load(slot, ref):
         return pltpu.make_async_copy(ref, pool.at[slot], load_sem.at[slot])
@@ -75,16 +75,20 @@
         load(A, y_ref).start()
         load(B, x_ref).start()
 
-    def send(src, dst, h, peer, sem=None):
-        at = pl.ds(h * half, half)
+    def transfer(src, dst, sent, received, peer):
         return pltpu.make_async_remote_copy(
-            src_ref=pool.at[src, at],
-            dst_ref=pool.at[dst, at],
-            send_sem=send_sem.at[dst if sem is None else sem, h],
-            recv_sem=recv_sem.at[dst, h],
-            device_id=(peer,),
-            device_id_type=MESH,
+            src_ref=src, dst_ref=dst, send_sem=sent, recv_sem=received, device_id=(peer,), device_id_type=MESH
         )
+
+    def copy(src, dst, at, sent, received, peer):
+        return transfer(pool.at[src, at], pool.at[dst, at], sent, received, peer)
+
+    def send(src, dst, h, peer):
+        return copy(src, dst, pl.ds(h * half, half), send_sem.at[dst, h], recv_sem.at[dst, h], peer)
+
+    def relay(src, h, piece, sent, peer):
+        at = pl.ds(h * half + piece * (half // 2), half // 2)
+        return copy(src, D3, at, send_sem.at[sent, h], recv_sem.at[(D3, A)[piece], h], peer)
 
     def send_a(h):
         return send(A, E2, h, front)
@@ -102,33 +106,49 @@
         return send(D2, E3, h, sib)
 
     def relay_d1(h):
-        return send(D1, D3, h, back)
+        return relay(D1, h, 0, D3, back)
 
     def relay_e2(h):
-        return send(E2, D3, h, before, A)
+        return relay(E2, h, 1, A, cross)
+
+    def stand_in(h):
+        return relay(E2, h, 0, B, cross)
 
     def start(which):
         which(0).start()
         which(1).start()
 
+    pl.semaphore_wait(barrier, jnp.where(opens, 2, jnp.where(early, 3, 4)))
+    pl.when(last)(lambda: pl.semaphore_signal(left_sem, inc=1, device_id=(right,), device_id_type=MESH))
+    pl.when(closes)(lambda: pl.semaphore_signal(left_sem, inc=1, device_id=(cross,), device_id_type=MESH))
+    behind = early | (last & (core == 0))
+
+    def start_from(ref, dst, peer):
+        for h in range(2):
+            at = pl.ds(h * half, half)
+            transfer(ref.at[at], pool.at[dst, at], send_sem.at[dst, h], recv_sem.at[dst, h], peer).start()
+
+    for parity, (a_ref, b_ref) in enumerate(((x_ref, y_ref), (y_ref, x_ref))):
+        here = core == parity
+        pl.when(here & jnp.logical_not(opens))(functools.partial(start_from, a_ref, E2, front))
+        pl.when(here & jnp.logical_not(behind))(functools.partial(start_from, b_ref, D2, back))
+        pl.when(here)(functools.partial(start_from, b_ref, SIB, sib))
     acc[...] = jnp.zeros_like(acc)
     scale[...] = jnp.exp(jnp.full(scale.shape, ls_ref[0], jnp.float32))
     offset = bias_ref[0]
     load(A, x_ref).wait()
     load(B, y_ref).wait()
-    pl.semaphore_wait(barrier, jnp.where(first, 2, jnp.where(closes, 4, 3)))
-    pl.when(last)(lambda: pl.semaphore_signal(left_sem, inc=1, device_id=(right,), device_id_type=MESH))
-    pl.when(closes)(lambda: pl.semaphore_signal(left_sem, inc=1, device_id=(after,), device_id_type=MESH))
-    pl.when(opens)(lambda: start(send_b))
-    pl.when(jnp.logical_not(opens))(lambda: start(send_a))
-    start(send_sib)
     for slot in range(2):
         high[slot], low[slot] = halves(pool[slot])
 
     def take_e2(h):
         send_a(h).wait_recv()
         pass_e2(h).start()
-        pl.when(opens)(lambda: relay_e2(h).start())
+        waits = opens | closes
+        pl.when(jnp.logical_not(waits))(lambda: relay_e2(h).start())
+        if h == 1:
+            pl.when(waits)(lambda: start(relay_e2))
+            pl.when(opens)(lambda: start(stand_in))
 
     def take_d2(h):
         send_b(h).wait_recv()
@@ -144,7 +164,7 @@
         pl.when(opens)(lambda: start(send_a))
 
     def start_later():
-        pl.when(jnp.logical_not(opens))(lambda: start(send_b))
+        pl.when(behind)(lambda: start(send_b))
 
     def add_pairs(mine, slot, h):
         at = pl.multiple_of(h * half, half)
@@ -170,7 +190,7 @@
     def recv(which, h):
         return lambda: which(h).wait_recv()
 
-    events = [(jnp.int32(LOCAL), open_left), (jnp.where(first, LOCAL + 2, LOCAL), start_later)]
+    events = [(jnp.int32(LOCAL), open_left), (jnp.int32(LOCAL), start_later)]
     for h in range(2):
         events += [
             (step_of(SIB, h), recv(send_sib, h)),
@@ -179,6 +199,7 @@
             (step_of(E3, h), recv(pass_d2, h)),
             (step_of(D1, h), functools.partial(take_d1, h)),
             (step_of(D3, h), recv(relay_d1, h)),
+            (step_of(D3, h), recv(relay_e2, h)),
         ]
 
     def by_order(i, part):
@@ -197,8 +218,9 @@
     for h in range(2):
         for which in (send_a, send_b, send_sib, pass_e2, pass_d2):
             which(h).wait_send()
+        relay_e2(h).wait_send()
         pl.when(jnp.logical_not(early))(lambda: relay_d1(h).wait_send())
-        pl.when(opens)(lambda: relay_e2(h).wait_send())
+        pl.when(opens)(lambda: stand_in(h).wait_send())
 
 
 def place(acc, xg_ref, yg_ref, sem):

time: 55 us -> 55 us (level)
  the two profiles are of different devices: /device:TPU:1 before, /device:TPU:0 now
where the time goes in v4:
time: 55 us; the launch traced here: 54.8 us
  Pallas kernels  52.9 us (96%)
  between operations  1.93 us (4%)
    pallas_call x1, Pallas kernels, per_device(): pl.pallas_call(functools.partial(kernel, n), out_shape=pltpu.VMEM((2, *bl...  51.5 us
    pallas_call x1, Pallas kernels, per_device(): pl.pallas_call(place, out_shape=(pltpu.HBM(block, jnp.float32),) * 2, in_...  1.43 us

profile of v4, /device:TPU:0, one launch (start us, length us, event | category | flops | bytes accessed | tf_op | source)
XLA Modules:
  0.0 54.8 jit_solution(3773644377241037994)
XLA Ops:
  1.9 51.5 %shard_map.59.acc = f32[2,256,1152]{2,1,0:T(8,128)S(1)} custom-call(f32[256,1152]{1,0:T(8,128)} %x_ref.1, f32[256,1152]{1,0:T(8,128)} %y_ref.1, f32[1]{0:T(128)S(6)} %copy.6.ls_ref, f32[1]{0:T(128)S(6)} %copy.7.bias_ref), custom_call_target="tpu_custom_call" | custom-call | tf_op jit(solution)/shard_map/pallas_call | solution.py:250
  53.4 1.4 %shard_map.60 = (f32[256,1152]{1,0:T(8,128)}, f32[256,1152]{1,0:T(8,128)}) custom-call(f32[2,256,1152]{2,1,0:T(8,128)S(1)} %shard_map.59.acc), custom_call_target="tpu_custom_call" | custom-call | tf_op jit(solution)/shard_map/pallas_call | solution.py:268

commit v5 on v4

--- a/solution.py
+++ b/solution.py
@@ -18,7 +18,7 @@
     START + ((D2, 0), (D1, 0), (E2, 0), (D2, 1), (E2, 1), (D1, 1), (E3, 0), (D3, 0), (E3, 1), (D3, 1)),
 )
 LAST = (
-    USUAL,
+    START + ((E2, 0), (D2, 0), (D1, 0), (D2, 1), (D1, 1), (E3, 0), (E2, 1), (E3, 1), (D3, 0), (D3, 1)),
     START + ((E2, 0), (D1, 0), (E3, 0), (D2, 0), (E2, 1), (D1, 1), (E3, 1), (D2, 1), (D3, 0), (D3, 1)),
 )
 

time: 55 us -> 53.8 us (0.978)
  Pallas kernels: 52.9 us -> 51.7 us
    pallas_call x1, Pallas kernels: 51.5 us -> 50.3 us  [per_device(): pl.pallas_call(functools.partial(kernel, n), out_shape=pltpu.VMEM((2, *bl...]
where the time goes in v5:
time: 53.8 us; the launch traced here: 53.7 us
  Pallas kernels  51.7 us (96%)
  between operations  1.93 us (4%)
    pallas_call x1, Pallas kernels, per_device(): pl.pallas_call(functools.partial(kernel, n), out_shape=pltpu.VMEM((2, *bl...  50.3 us
    pallas_call x1, Pallas kernels, per_device(): pl.pallas_call(place, out_shape=(pltpu.HBM(block, jnp.float32),) * 2, in_...  1.43 us

profile of v5, /device:TPU:0, one launch (start us, length us, event | category | flops | bytes accessed | tf_op | source)
XLA Modules:
  0.0 53.7 jit_solution(8459604500184065430)
XLA Ops:
  1.9 50.3 %shard_map.59.acc = f32[2,256,1152]{2,1,0:T(8,128)S(1)} custom-call(f32[256,1152]{1,0:T(8,128)} %x_ref.1, f32[256,1152]{1,0:T(8,128)} %y_ref.1, f32[1]{0:T(128)S(6)} %copy.6.ls_ref, f32[1]{0:T(128)S(6)} %copy.7.bias_ref), custom_call_target="tpu_custom_call" | custom-call | tf_op jit(solution)/shard_map/pallas_call | solution.py:250
  52.2 1.4 %shard_map.60 = (f32[256,1152]{1,0:T(8,128)}, f32[256,1152]{1,0:T(8,128)}) custom-call(f32[2,256,1152]{2,1,0:T(8,128)S(1)} %shard_map.59.acc), custom_call_target="tpu_custom_call" | custom-call | tf_op jit(solution)/shard_map/pallas_call | solution.py:268

commit v6 on v5

--- a/solution.py
+++ b/solution.py
@@ -19,7 +19,7 @@
 )
 LAST = (
     START + ((E2, 0), (D2, 0), (D1, 0), (D2, 1), (D1, 1), (E3, 0), (E2, 1), (E3, 1), (D3, 0), (D3, 1)),
-    START + ((E2, 0), (D1, 0), (E3, 0), (D2, 0), (E2, 1), (D1, 1), (E3, 1), (D2, 1), (D3, 0), (D3, 1)),
+    START + ((E2, 0), (D1, 0), (E3, 0), (E2, 1), (D2, 0), (D1, 1), (E3, 1), (D2, 1), (D3, 0), (D3, 1)),
 )
 
 
@@ -59,8 +59,9 @@
     opens, early, closes = first & (core == 0), first & (core == 1), last & (core == 1)
     greet(sib)
     greet(left)
-    pl.when(jnp.logical_not(last))(lambda: greet(right))
-    pl.when(jnp.logical_not(closes))(lambda: greet(cross))
+    near, ends = chip == n // 2 - 2, last & (core == 0)
+    pl.when(jnp.logical_not(last | near))(lambda: greet(right))
+    pl.when(jnp.logical_not(closes | (near & (core == 1))))(lambda: greet(cross))
 
     def load(slot, ref):
         return pltpu.make_async_copy(ref, pool.at[slot], load_sem.at[slot])
@@ -118,10 +119,10 @@
         which(0).start()
         which(1).start()
 
-    pl.semaphore_wait(barrier, jnp.where(opens, 2, jnp.where(early, 3, 4)))
-    pl.when(last)(lambda: pl.semaphore_signal(left_sem, inc=1, device_id=(right,), device_id_type=MESH))
-    pl.when(closes)(lambda: pl.semaphore_signal(left_sem, inc=1, device_id=(cross,), device_id_type=MESH))
-    behind = early | (last & (core == 0))
+    pl.semaphore_wait(barrier, jnp.where(opens | ends, 2, jnp.where(early | closes, 3, 4)))
+    pl.when(last | near)(lambda: pl.semaphore_signal(left_sem, inc=1, device_id=(right,), device_id_type=MESH))
+    pl.when(closes | (near & (core == 1)))(lambda: pl.semaphore_signal(left_sem, inc=1, device_id=(cross,), device_id_type=MESH))
+    behind = early | ends
 
     def start_from(ref, dst, peer):
         for h in range(2):
@@ -130,9 +131,20 @@
 
     for parity, (a_ref, b_ref) in enumerate(((x_ref, y_ref), (y_ref, x_ref))):
         here = core == parity
-        pl.when(here & jnp.logical_not(opens))(functools.partial(start_from, a_ref, E2, front))
-        pl.when(here & jnp.logical_not(behind))(functools.partial(start_from, b_ref, D2, back))
+        pl.when(here & jnp.logical_not(opens | ends))(functools.partial(start_from, a_ref, E2, front))
+        pl.when(here & jnp.logical_not(behind | closes))(functools.partial(start_from, b_ref, D2, back))
         pl.when(here)(functools.partial(start_from, b_ref, SIB, sib))
+
+    @pl.when(ends)
+    def _():
+        pl.semaphore_wait(left_sem, 2)
+        start_from(x_ref, E2, front)
+
+    @pl.when(closes)
+    def _():
+        pl.semaphore_wait(left_sem, 1)
+        start_from(x_ref, D2, back)
+
     acc[...] = jnp.zeros_like(acc)
     scale[...] = jnp.exp(jnp.full(scale.shape, ls_ref[0], jnp.float32))
     offset = bias_ref[0]

time: 53.8 us -> 53.8 us (level)
  no operation moved by 1% of the time
where the time goes in v6:
time: 53.8 us; the launch traced here: 53.7 us
  Pallas kernels  51.7 us (96%)
  between operations  1.93 us (4%)
    pallas_call x1, Pallas kernels, per_device(): pl.pallas_call(functools.partial(kernel, n), out_shape=pltpu.VMEM((2, *bl...  50.3 us
    pallas_call x1, Pallas kernels, per_device(): pl.pallas_call(place, out_shape=(pltpu.HBM(block, jnp.float32),) * 2, in_...  1.43 us

profile of v6, /device:TPU:0, one launch (start us, length us, event | category | flops | bytes accessed | tf_op | source)
XLA Modules:
  0.0 53.7 jit_solution(13802347301039097543)
XLA Ops:
  1.9 50.3 %shard_map.59.acc = f32[2,256,1152]{2,1,0:T(8,128)S(1)} custom-call(f32[256,1152]{1,0:T(8,128)} %x_ref.1, f32[256,1152]{1,0:T(8,128)} %y_ref.1, f32[1]{0:T(128)S(6)} %copy.6.ls_ref, f32[1]{0:T(128)S(6)} %copy.7.bias_ref), custom_call_target="tpu_custom_call" | custom-call | tf_op jit(solution)/shard_map/pallas_call | solution.py:262
  52.2 1.4 %shard_map.60 = (f32[256,1152]{1,0:T(8,128)}, f32[256,1152]{1,0:T(8,128)}) custom-call(f32[2,256,1152]{2,1,0:T(8,128)S(1)} %shard_map.59.acc), custom_call_target="tpu_custom_call" | custom-call | tf_op jit(solution)/shard_map/pallas_call | solution.py:280
